TPU v7x, 32 devices: a whole 2x2x4 slice. The times are simulated.
32 devices in a mesh: uly: 4 (over x, core), blk: 8 (over z, y).
Axes of the slice: x: 2, y: 2, z: 4, core: 2. Of those that a mesh axis runs over, the one named last changes fastest.
Arguments:
- tokens: bfloat16 [8, 512, 3072], P('blk', 'uly'), may hold values from -18 to 18
- query_weight: bfloat16 [3072, 32, 128], P('blk', 'uly'), may hold values from -0.109375 to 0.109375
- key_values: bfloat16 [8, 512, 32, 256], P('blk', 'uly'), may hold values from -18 to 18
Outputs:
- attended: bfloat16 [8, 512, 32, 128], P('blk', 'uly')
All inputs are finite; a program needn't handle non-finite values.
Results may differ from a plain program's by a relative error of at most 0.012.
Values may be sent and summed in bfloat16 or wider, within the bound.
A program may use at most 64 MiB of HBM per device.

v0:
```python
import jax
import jax.numpy as jnp
from jax import lax
from jax.sharding import PartitionSpec as P


def attend_heads(queries, head_kv, head_width):
    row_count = queries.shape[0]
    head_count = queries.shape[1]
    key_rows = head_kv[:, :, :head_width]
    value_rows = head_kv[:, :, head_width:]
    score_scale = head_width ** (-0.5)
    block_rows = min(512, row_count)
    query_blocks = queries.reshape(row_count // block_rows, block_rows, head_count, head_width)

    def attend(query_block):
        scores = (
            jnp.einsum("qhd,khd->hqk", query_block, key_rows, preferred_element_type=jnp.float32)
            * score_scale
        )
        row_max = jnp.max(scores, axis=2, keepdims=True)
        soft = jnp.exp(scores - row_max)
        row_sum = jnp.sum(soft, axis=2)
        weighted = jnp.einsum(
            "hqk,khd->qhd",
            soft.astype(jnp.bfloat16),
            value_rows,
            preferred_element_type=jnp.float32,
        )
        return (weighted / jnp.transpose(row_sum)[:, :, None]).astype(jnp.bfloat16)

    return lax.map(attend, query_blocks).reshape(row_count, head_count, head_width)


def body(tokens, query_weight, key_values):
    local_tokens = tokens[0]
    shard_rows = query_weight.shape[0]
    head_count = query_weight.shape[1]
    head_width = query_weight.shape[2]
    flat_weight = query_weight.reshape(shard_rows, head_count * head_width)
    gathered = lax.all_gather(local_tokens, "uly", axis=0, tiled=True)
    projected = jnp.dot(
        gathered,
        lax.all_gather(flat_weight, "blk", axis=0, tiled=True),
        preferred_element_type=jnp.float32,
    )
    row_count = projected.shape[0]
    queries = projected.astype(jnp.bfloat16).reshape(row_count, head_count, head_width)
    head_kv = lax.all_to_all(key_values[0], "uly", split_axis=1, concat_axis=0, tiled=True)
    normalized = attend_heads(queries, head_kv, head_width)
    returned = lax.all_to_all(normalized, "uly", split_axis=0, concat_axis=1, tiled=True)
    return returned[None]


def solution(mesh):
    return jax.shard_map(
        body,
        mesh=mesh,
        in_specs=(P("blk", "uly", None), P("blk", "uly", None), P("blk", "uly", None, None)),
        out_specs=P("blk", "uly", None, None),
        check_vma=False,
    )
```

profile of v0, /device:TPU:0, one launch (start us, length us, event | category | flops | bytes accessed | tf_op | source)
XLA Modules:
  0.0 196.3 jit_solution(10798446490265880210)
XLA Ops:
  6.5 0.0 all-gather.6.cloned.1.call-start
  6.5 0.7 all-gather.6.cloned.1.call-update
  7.3 0.0 all-gather.4.cloned.1.call-start
  7.3 2.2 %copy.28 = bf16[48,8,8,128]{3,1,2,0:T(8,128)(2,1)} copy(bf16[48,8,8,128]{3,2,1,0:T(8,128)(2,1)} %bitcast.43) | data formatting | bytes 1572864
  9.5 0.0 all-gather.4.cloned.1.call-update
  9.5 2.8 %copy.26 = bf16[1,128,32,256]{3,1,2,0:T(8,128)(2,1)S(1)} copy(bf16[1,128,32,256]{3,2,1,0:T(8,128)(2,1)} %param.5) | data formatting | bytes 4194304 | tf_op args[2]
  12.3 46.6 %all_to_all.33 = bf16[128,32,256]{2,0,1:T(8,128)(2,1)S(1)} all-to-all(bf16[128,32,256]{2,0,1:T(8,128)(2,1)S(1)} %bitcast.38), channel_id=1, replica_groups=mesh['uly'=4,'blk'=8] {'uly'}, dimensions={1} | all-to-all | bytes 4194304 | tf_op jit(solution)/shard_map/all_to_all | solution.py:49
  58.9 0.1 copy.9
  59.0 0.0 all-gather.6.cloned.1.call-done
  59.0 99.4 %all-gather.4.cloned.1.call-done = bf16[3072,1024]{1,0:T(8,128)(2,1)} async-done(((bf16[384,1024]{1,0:T(8,128)(2,1)}), bf16[3072,1024]{1,0:T(8,128)(2,1)}) %all-gather.4.cloned.1.call-update) | async-done | bytes 6291472 | tf_op jit(solution)/shard_map/all_gather | solution.py:44
  158.4 7.2 %fusion.14 = bf16[64,8,8,128]{3,2,1,0:T(8,128)(2,1)S(1)} fusion(bf16[3072,1024]{1,0:T(8,128)(2,1)} %all-gather.4.cloned.1.call-done, bf16[1,512,3072]{2,1,0:T(8,128)(2,1)} %all-gather.6.cloned.1.call-done), kind=kOutput, calls=%fused_computation.13 | convolution fusion | flops 3221749760 | bytes 10485760 | tf_op jit(solution)/shard_map/dot_general | solution.py:42
  165.6 1.3 multiply_reduce_fusion
  166.8 1.4 fusion
  168.2 2.4 %fusion.8 = bf16[512,8,128]{2,0,1:T(8,128)(2,1)S(1)} fusion(f32[8,512,512]{1,2,0:T(8,128)S(1)} %get-tuple-element.14, f32[8,512]{1,0:T(8,128)S(1)} %get-tuple-element.13, bf16[512,8,256]{2,0,1:T(8,128)(2,1)S(1)} %bitcast.40, f32[512,8]{0,1:T(8,128)S(1)} %bitcast.44), kind=kOutput, calls=%fused_computation.10 | convolution fusion | flops 544210944 | bytes 10518528 | tf_op jit(solution)/shard_map/while/body/eval_jaxpr/hqk,khd->qhd/dot_general | solution.py:24
  170.6 0.7 copy.12
  171.3 17.0 %all_to_all.34 = bf16[512,8,128]{2,1,0:T(8,128)(2,1)S(1)} all-to-all(bf16[512,8,128]{2,1,0:T(8,128)(2,1)S(1)} %copy.12), channel_id=1, replica_groups=mesh['uly'=4,'blk'=8] {'uly'}, dimensions={0} | all-to-all | bytes 2097152 | tf_op jit(solution)/shard_map/all_to_all | solution.py:51
  188.3 1.1 copy.27
Async XLA Ops:
  6.5 52.5 %all-gather.6.cloned.1.call-start = ((), (), s32[]{:S(2)}) async-start(), calls=%async_computation.3 | async-start | bytes 3932160 | tf_op jit(solution)/shard_map/all_gather | solution.py:41
  7.3 151.1 %all-gather.4.cloned.1.call-start = ((), (), s32[]{:S(2)}) async-start(), calls=%async_computation.2 | async-start | bytes 7077888 | tf_op jit(solution)/shard_map/all_gather | solution.py:44
Sparse Core Ops, SparseCore 0:
  8.9 48.1 all-gather.5
  59.3 99.0 all-gather.3
where the time goes:
time: 197 us; the launch traced here: 196 us
  waiting for transfers between devices  100 us (51%)
  blocking collectives  63.6 us (32%)
  between operations  13.4 us (7%)
  matrix products  10.8 us (5%)
  local copies, waits for them, and re-layouts  6.93 us (4%)
    all_gather x1, waiting for transfers between devices, body(): lax.all_gather(flat_weight, 'blk', axis=0, tiled=True)  99.4 us
    all_to_all x1, blocking collectives, body(): lax.all_to_all(key_values[0], 'uly', split_axis=1, concat_axis=0, tiled=T...  46.6 us
    all_to_all x1, blocking collectives, body(): lax.all_to_all(normalized, 'uly', split_axis=0, concat_axis=1, tiled=True)  17 us
    dot_general x1, matrix products, body(): jnp.dot(gathered, lax.all_gather(flat_weight, 'blk', axis=0, tiled=True),...  7.15 us
    unnamed x2, local copies, waits for them, and re-layouts  4.96 us
  transfers between devices with their start and end apart: 2, of which 1 were waited for; matrix products, arithmetic and copies ran while one was open for 3% of the time, Pallas kernels for 0%

commit v1 on v0

v1 whole, which is shorter than its diff:
```python
import functools

import jax
import jax.numpy as jnp
from jax import lax
from jax.experimental import pallas as pl
from jax.experimental.pallas import tpu as pltpu
from jax.sharding import PartitionSpec as P

MESH = pl.DeviceIdType.MESH
CHUNK_HEADS = 2
QUERY_ROWS = 256


def kernel(
    n,
    blocks,
    head_width,
    chunks,
    tok_in,
    w_in,
    kv_in,
    out_ref,
    tok,
    wbuf,
    kvbuf,
    att,
    qbuf,
    loc_sem,
    tok_send,
    tok_fwd,
    tok_recv,
    w_send,
    w_recv,
    kv_send,
    kv_recv,
    out_send,
    out_recv,
    out_loc,
):
    u = lax.axis_index("uly")
    b = lax.axis_index("blk")
    line = blocks // 2
    z = b // 2
    y = b % 2
    mate = z * 2 + (1 - y)
    core_mate = u + 1 - 2 * (u % 2)
    seq_rows = tok_in.shape[0]
    shard = w_in.shape[0]
    width = w_in.shape[1]
    cols = width // chunks
    kv_width = 2 * width
    kv_cols = 2 * cols
    total_rows = n * seq_rows

    def ds(start, size):
        return pl.ds(pl.multiple_of(start * size, size), size)

    def remote(src, dst, send, recv, device):
        return pltpu.make_async_remote_copy(
            src_ref=src, dst_ref=dst, send_sem=send, recv_sem=recv,
            device_id=device, device_id_type=MESH,
        )

    has_up = z < line - 1
    has_down = z > 0

    barrier = pltpu.get_barrier_semaphore()

    def greet(device):
        pl.semaphore_signal(barrier, inc=1, device_id=device, device_id_type=MESH)

    for k in range(1, n):
        greet({"uly": (u + k) % n})
    greet({"blk": mate})

    @pl.when(has_up)
    def _():
        greet({"blk": b + 2})

    @pl.when(has_down)
    def _():
        greet({"blk": b - 2})

    inner = jnp.logical_and(has_up, has_down)

    @pl.when(inner)
    def _():
        pl.semaphore_wait(barrier, n + 2)

    @pl.when(jnp.logical_and(jnp.logical_not(inner), jnp.logical_or(has_up, has_down)))
    def _():
        pl.semaphore_wait(barrier, n + 1)

    @pl.when(jnp.logical_not(jnp.logical_or(has_up, has_down)))
    def _():
        pl.semaphore_wait(barrier, n)

    def piece(c, s):
        return wbuf.at[ds(s, shard), ds(c, cols)]

    UP, DOWN, ACROSS = 0, 1, 2

    def w_copy(c, s, way, own=False):
        step = (2, -2, 0)[way]
        device = mate if way == ACROSS else b + step
        src = w_in.at[:, ds(c, cols)] if own else piece(c, s)
        return remote(src, piece(c, s), w_send.at[way, c, s], w_recv.at[c, s], {"blk": device})

    def own_weights(c):
        w_copy(c, b, ACROSS, True).start()

        @pl.when(has_up)
        def _():
            w_copy(c, b, UP, True).start()

        @pl.when(has_down)
        def _():
            w_copy(c, b, DOWN, True).start()

    def pass_on(c):
        for d in range(1, line):
            @pl.when(z - d >= 0)
            def _():
                s = b - 2 * d
                w_copy(c, s, ACROSS).wait_recv()

                @pl.when(has_up)
                def _():
                    w_copy(c, s, UP).start()

                w_copy(c, s, ACROSS).start()

            @pl.when(z + d < line)
            def _():
                s = b + 2 * d
                w_copy(c, s, ACROSS).wait_recv()

                @pl.when(has_down)
                def _():
                    w_copy(c, s, DOWN).start()

                w_copy(c, s, ACROSS).start()

    def across_arrived(c):
        for j in range(line):
            w_copy(c, 2 * j + 1 - y, ACROSS).wait_recv()

    def weights_sent(c):
        for j in range(line):
            s = 2 * j + y
            w_copy(c, s, ACROSS).wait_send()

            @pl.when(jnp.logical_and(has_up, j <= z))
            def _():
                w_copy(c, s, UP).wait_send()

            @pl.when(jnp.logical_and(has_down, j >= z))
            def _():
                w_copy(c, s, DOWN).wait_send()

    def token_rows(s):
        return tok.at[ds(s, seq_rows), :]

    def token_copy(k):
        return remote(tok_in, token_rows(u), tok_send.at[k], tok_recv.at[u], {"uly": (u + k) % n})

    def token_mate():
        return remote(tok_in, token_rows(u), tok_send.at[1], tok_recv.at[u], {"uly": core_mate})

    def token_forward(k):
        s = (u + n - k) % n
        return remote(token_rows(s), token_rows(s), tok_fwd.at[k], tok_recv.at[s], {"uly": core_mate})

    def token_arrival(s):
        return remote(token_rows(s), token_rows(s), tok_fwd.at[0], tok_recv.at[s], {"uly": core_mate})

    def kv_copy(c, k):
        to = (u + k) % n
        src = kv_in.at[:, pl.ds(pl.multiple_of(to * kv_width + c * kv_cols, kv_cols), kv_cols)]
        dst = kvbuf.at[ds(u, seq_rows), ds(c, kv_cols)]
        return remote(src, dst, kv_send.at[c, k], kv_recv.at[c, u], {"uly": to})

    def kv_arrival(c, k):
        s = (u + n - k) % n
        dst = kvbuf.at[ds(s, seq_rows), ds(c, kv_cols)]
        return remote(dst, dst, kv_send.at[c, k], kv_recv.at[c, s], {"uly": s})

    def out_place(s, c):
        return out_ref.at[:, pl.ds(pl.multiple_of(s * width + c * cols, cols), cols)]

    def out_copy(c, k):
        to = (u + k) % n
        src = att.at[ds(to, seq_rows), ds(c, cols)]
        return remote(src, out_place(u, c), out_send.at[c, k], out_recv.at[c, u], {"uly": to})

    def out_arrival(c, k):
        s = (u + n - k) % n
        src = att.at[ds(s, seq_rows), ds(c, cols)]
        return remote(src, out_place(s, c), out_send.at[c, k], out_recv.at[c, s], {"uly": s})

    def out_own(c):
        return pltpu.make_async_copy(att.at[ds(u, seq_rows), ds(c, cols)], out_place(u, c), out_loc.at[c])

    own_weights(0)
    for k in range(2, n, 2):
        token_copy(k).start()
    token_mate().start()
    for k in range(1, n):
        kv_copy(0, k).start()
    locals_ = (
        pltpu.make_async_copy(w_in, wbuf.at[ds(b, shard), :], loc_sem.at[0]),
        pltpu.make_async_copy(tok_in, token_rows(u), loc_sem.at[1]),
        pltpu.make_async_copy(
            kv_in.at[:, ds(u, kv_width)], kvbuf.at[ds(u, seq_rows), :], loc_sem.at[2]
        ),
    )
    for copy in locals_:
        copy.start()
    for copy in locals_:
        copy.wait()

    scale = head_width ** (-0.5)
    block = min(QUERY_ROWS, total_rows)

    def attend(c):
        def rows_step(r, carry):
            rows = pl.ds(pl.multiple_of(r * block, block), block)
            qbuf[rows, :] = jnp.dot(
                tok[rows, :], wbuf[:, ds(c, cols)], preferred_element_type=jnp.float32
            ).astype(jnp.bfloat16)
            for h in range(cols // head_width):
                q = qbuf[rows, h * head_width:(h + 1) * head_width]
                at = c * kv_cols + 2 * h * head_width
                k = kvbuf[:, pl.ds(pl.multiple_of(at, head_width), head_width)]
                v = kvbuf[:, pl.ds(pl.multiple_of(at + head_width, head_width), head_width)]
                scores = lax.dot_general(
                    q, k, (((1,), (1,)), ((), ())), preferred_element_type=jnp.float32
                ) * scale
                soft = jnp.exp(scores - jnp.max(scores, axis=1, keepdims=True))
                row_sum = jnp.sum(soft, axis=1, keepdims=True)
                weighted = jnp.dot(
                    soft.astype(jnp.bfloat16), v, preferred_element_type=jnp.float32
                )
                place = pl.ds(pl.multiple_of(c * cols + h * head_width, head_width), head_width)
                att[rows, place] = (weighted / row_sum).astype(jnp.bfloat16)
            return carry

        lax.fori_loop(0, total_rows // block, rows_step, 0)

    def chunk_step(i, carry):
        @pl.when(i + 1 < chunks)
        def _():
            own_weights(i + 1)

        @pl.when(i < chunks)
        def _():
            pass_on(i)

        @pl.when(i == 0)
        def _():
            for k in range(2, n, 2):
                token_arrival((u + n - k) % n).wait_recv()
                token_forward(k).start()
            for k in range(1, n, 2):
                token_arrival((u + n - k) % n).wait_recv()

        @pl.when(i + 1 < chunks)
        def _():
            for k in range(1, n):
                kv_copy(i + 1, k).start()

        @pl.when(i > 0)
        def _():
            c = i - 1
            across_arrived(c)
            for k in range(1, n):
                kv_arrival(c, k).wait_recv()
            attend(c)
            for k in range(1, n):
                out_copy(c, k).start()
            out_own(c).start()

        return carry

    lax.fori_loop(0, chunks + 1, chunk_step, 0)

    def drain(c, carry):
        weights_sent(c)
        for k in range(1, n):
            kv_copy(c, k).wait_send()
            out_copy(c, k).wait_send()
            out_arrival(c, k).wait_recv()
        out_own(c).wait()
        return carry

    lax.fori_loop(0, chunks, drain, 0)
    for k in range(2, n, 2):
        token_copy(k).wait_send()
        token_forward(k).wait_send()
    token_mate().wait_send()


def body(n, blocks, tokens, query_weight, key_values):
    seq_rows, depth = tokens.shape[1:]
    shard, heads, head_width = query_weight.shape
    all_heads = key_values.shape[2]
    width = heads * head_width
    chunk_heads = CHUNK_HEADS if heads % CHUNK_HEADS == 0 else 1
    chunks = heads // chunk_heads
    cols = width // chunks
    total_rows = n * seq_rows
    dma = pltpu.SemaphoreType.DMA
    flops = 2 * total_rows * width * (depth + 2 * total_rows)
    out = pl.pallas_call(
        functools.partial(kernel, n, blocks, head_width, chunks),
        out_shape=jax.ShapeDtypeStruct((seq_rows, all_heads * head_width), jnp.bfloat16),
        in_specs=[pl.BlockSpec(memory_space=pl.ANY)] * 3,
        out_specs=pl.BlockSpec(memory_space=pl.ANY),
        scratch_shapes=[
            pltpu.VMEM((total_rows, depth), jnp.bfloat16),
            pltpu.VMEM((depth, width), jnp.bfloat16),
            pltpu.VMEM((total_rows, 2 * width), jnp.bfloat16),
            pltpu.VMEM((total_rows, width), jnp.bfloat16),
            pltpu.VMEM((total_rows, cols), jnp.bfloat16),
            dma((3,)),
            dma((n,)),
            dma((n,)),
            dma((n,)),
            dma((3, chunks, blocks)),
            dma((chunks, blocks)),
            dma((chunks, n)),
            dma((chunks, n)),
            dma((chunks, n)),
            dma((chunks, n)),
            dma((chunks,)),
        ],
        compiler_params=pltpu.CompilerParams(
            collective_id=0, has_side_effects=True, vmem_limit_bytes=48 * 1024 * 1024
        ),
        cost_estimate=pl.CostEstimate(
            flops=flops,
            bytes_accessed=2 * (tokens.size + query_weight.size + key_values.size),
            transcendentals=total_rows * total_rows * heads,
        ),
    )(
        tokens[0],
        query_weight.reshape(shard, width),
        key_values[0].reshape(seq_rows, all_heads * 2 * head_width),
    )
    return out.reshape(1, seq_rows, all_heads, head_width)


def solution(mesh):
    return jax.shard_map(
        functools.partial(body, mesh.shape["uly"], mesh.shape["blk"]),
        mesh=mesh,
        in_specs=(P("blk", "uly", None), P("blk", "uly", None), P("blk", "uly", None, None)),
        out_specs=P("blk", "uly", None, None),
        check_vma=False,
    )
```

time: 197 us -> 92.8 us (0.47)
  waiting for transfers between devices: 100 us -> 0 us
  Pallas kernels: 0 us -> 86.7 us
  blocking collectives: 63.6 us -> 0 us
  between operations: 13.4 us -> 0.03 us
  matrix products: 10.8 us -> 0 us
    all_gather x2 -> x0, waiting for transfers between devices: 99.4 us -> none  [the longest x1 99.4 us: body(): lax.all_gather(flat_weight, 'blk', axis=0, tiled=True)]
    pallas_call x0 -> x1, Pallas kernels: none -> 86.7 us  [body(): pl.pallas_call(functools.partial(kernel, n, blocks, head_width, chunks),...]
    all_to_all x2 -> x0, blocking collectives: 63.6 us -> none  [the longest x1 46.6 us: body(): lax.all_to_all(key_values[0], 'uly', split_axis=1, concat_axis=0, tiled=T...]
    dot_general x3 -> x0, matrix products: 10.8 us -> none  [the longest x1 7.15 us: body(): jnp.dot(gathered, lax.all_gather(flat_weight, 'blk', axis=0, tiled=True),...]
    unnamed x2 -> x5, local copies, waits for them, and re-layouts: 4.96 us -> 5.59 us
  transfers between devices with their start and end apart: 2 -> 0, of which waited for: 1 -> 0; matrix products, arithmetic and copies ran while one was open for 3% -> 0% of each run, Pallas kernels for 0% -> 0%
where the time goes in v1:
time: 92.8 us; the launch traced here: 92.3 us
  Pallas kernels  86.7 us (93%)
  local copies, waits for them, and re-layouts  5.59 us (6%)
    pallas_call x1, Pallas kernels, body(): pl.pallas_call(functools.partial(kernel, n, blocks, head_width, chunks),...  86.7 us
    unnamed x5, local copies, waits for them, and re-layouts  5.59 us

profile of v1, /device:TPU:0, one launch (start us, length us, event | category | flops | bytes accessed | tf_op | source)
XLA Modules:
  0.0 92.3 jit_solution(8005618172221880001)
XLA Ops:
  0.0 1.3 %copy.8 = bf16[48,8,8,128]{3,1,2,0:T(8,128)(2,1)S(1)} copy(bf16[48,8,8,128]{3,2,1,0:T(8,128)(2,1)} %bitcast.16) | data formatting | bytes 1572864
  1.3 0.0 copy-start
  1.3 3.1 %copy.5 = bf16[16,8,32,256]{3,1,2,0:T(8,128)(2,1)S(1)} copy(bf16[16,8,32,256]{3,2,1,0:T(8,128)(2,1)} %bitcast.15) | data formatting | bytes 4194304
  4.4 0.0 copy-done
  4.4 86.7 %shard_map.37 = bf16[128,4096]{1,0:T(8,128)(2,1)S(1)} custom-call(bf16[128,3072]{1,0:T(8,128)(2,1)S(1)} %bitcast.14, bf16[384,1024]{1,0:T(8,128)(2,1)S(1)} %bitcast.13, bf16[128,8192]{1,0:T(8,128)(2,1)S(1)} %bitcast.11), custom_call_target="tpu_custom_call" | custom-call | flops 4294967296 | bytes 3670016 | tf_op jit(solution)/shard_map/pallas_call | solution.py:315
  91.2 1.2 %copy.6 = bf16[16,8,32,128]{3,2,1,0:T(8,128)(2,1)} copy(bf16[16,8,32,128]{3,1,2,0:T(8,128)(2,1)S(1)} %bitcast.12) | data formatting | bytes 2097152
Async XLA Ops:
  1.3 3.1 %copy-start = (bf16[1,128,3072]{2,1,0:T(8,128)(2,1)S(1)}, bf16[1,128,3072]{2,1,0:T(8,128)(2,1)}, u32[]{:S(2)}) copy-start(bf16[1,128,3072]{2,1,0:T(8,128)(2,1)} %param.3) | copy-start | bytes 2359300

commit v2 on v1

--- a/solution.py
+++ b/solution.py
@@ -8,7 +8,8 @@
 from jax.sharding import PartitionSpec as P
 
 MESH = pl.DeviceIdType.MESH
-CHUNK_HEADS = 2
+CHUNK_HEADS = 1
+AHEAD = 2
 QUERY_ROWS = 256
 
 
@@ -26,12 +27,17 @@
     kvbuf,
     att,
     qbuf,
+    kv_raw,
+    kv_wide,
+    kv_flat,
     loc_sem,
     tok_send,
     tok_fwd,
     tok_recv,
     w_send,
     w_recv,
+    side_send,
+    side_recv,
     kv_send,
     kv_recv,
     out_send,
@@ -49,6 +55,7 @@
     shard = w_in.shape[0]
     width = w_in.shape[1]
     cols = width // chunks
+    side = max(16, shard // 6 // 16 * 16)
     kv_width = 2 * width
     kv_cols = 2 * cols
     total_rows = n * seq_rows
@@ -65,6 +72,15 @@
     has_up = z < line - 1
     has_down = z > 0
 
+    raw_copy = pltpu.make_async_copy(kv_in, kv_raw, loc_sem.at[3])
+    raw_copy.start()
+    own_copies = (
+        pltpu.make_async_copy(w_in, wbuf.at[ds(b, shard), :], loc_sem.at[0]),
+        pltpu.make_async_copy(tok_in, tok.at[ds(u, seq_rows), :], loc_sem.at[1]),
+    )
+    for copy in own_copies:
+        copy.start()
+
     barrier = pltpu.get_barrier_semaphore()
 
     def greet(device):
@@ -107,6 +123,16 @@
         src = w_in.at[:, ds(c, cols)] if own else piece(c, s)
         return remote(src, piece(c, s), w_send.at[way, c, s], w_recv.at[c, s], {"blk": device})
 
+    def main_copy(c, s):
+        rows = pl.ds(pl.multiple_of(s * shard + side, 16), shard - side)
+        part = wbuf.at[rows, ds(c, cols)]
+        return remote(part, part, w_send.at[ACROSS, c, s], w_recv.at[c, s], {"blk": mate})
+
+    def side_copy(c, s, way):
+        part = wbuf.at[pl.ds(pl.multiple_of(s * shard, 16), side), ds(c, cols)]
+        device = b + (2, -2)[way]
+        return remote(part, part, side_send.at[way, c, s], side_recv.at[c, s], {"blk": device})
+
     def own_weights(c):
         w_copy(c, b, ACROSS, True).start()
 
@@ -119,45 +145,74 @@
             w_copy(c, b, DOWN, True).start()
 
     def pass_on(c):
-        for d in range(1, line):
-            @pl.when(z - d >= 0)
-            def _():
-                s = b - 2 * d
-                w_copy(c, s, ACROSS).wait_recv()
-
-                @pl.when(has_up)
-                def _():
-                    w_copy(c, s, UP).start()
-
-                w_copy(c, s, ACROSS).start()
-
-            @pl.when(z + d < line)
-            def _():
-                s = b + 2 * d
-                w_copy(c, s, ACROSS).wait_recv()
-
-                @pl.when(has_down)
-                def _():
-                    w_copy(c, s, DOWN).start()
-
-                w_copy(c, s, ACROSS).start()
+        ways = lambda d: (
+            (UP, -2 * d, z - d >= 0, has_up),
+            (DOWN, 2 * d, z + d < line, has_down),
+        )
+
+        def main(d):
+            for way, step, there, more in ways(d):
+                @pl.when(there)
+                def _(way=way, step=step, more=more):
+                    w_copy(c, b + step, ACROSS).wait_recv()
+
+                    @pl.when(more)
+                    def _():
+                        w_copy(c, b + step, way).start()
+
+                    main_copy(c, b + step).start()
+
+        def sides(d):
+            for way, step, there, more in ways(d):
+                @pl.when(there)
+                def _(way=way, step=step, more=more):
+                    side_copy(c, mate + step, way).wait_recv()
+
+                    @pl.when(more)
+                    def _():
+                        side_copy(c, mate + step, way).start()
+
+        main(1)
+        w_copy(c, mate, ACROSS).wait_recv()
+
+        @pl.when(has_up)
+        def _():
+            side_copy(c, mate, UP).start()
+
+        @pl.when(has_down)
+        def _():
+            side_copy(c, mate, DOWN).start()
+
+        for d in range(2, line):
+            main(d)
+            sides(d - 1)
+        sides(line - 1)
 
     def across_arrived(c):
         for j in range(line):
-            w_copy(c, 2 * j + 1 - y, ACROSS).wait_recv()
+            @pl.when(j != z)
+            def _():
+                main_copy(c, 2 * j + 1 - y).wait_recv()
 
     def weights_sent(c):
+        w_copy(c, b, ACROSS).wait_send()
         for j in range(line):
             s = 2 * j + y
-            w_copy(c, s, ACROSS).wait_send()
+            other = 2 * j + 1 - y
+
+            @pl.when(j != z)
+            def _():
+                main_copy(c, s).wait_send()
 
             @pl.when(jnp.logical_and(has_up, j <= z))
             def _():
                 w_copy(c, s, UP).wait_send()
+                side_copy(c, other, UP).wait_send()
 
             @pl.when(jnp.logical_and(has_down, j >= z))
             def _():
                 w_copy(c, s, DOWN).wait_send()
+                side_copy(c, other, DOWN).wait_send()
 
     def token_rows(s):
         return tok.at[ds(s, seq_rows), :]
@@ -177,7 +232,7 @@
 
     def kv_copy(c, k):
         to = (u + k) % n
-        src = kv_in.at[:, pl.ds(pl.multiple_of(to * kv_width + c * kv_cols, kv_cols), kv_cols)]
+        src = kv_flat.at[:, pl.ds(pl.multiple_of(to * kv_width + c * kv_cols, kv_cols), kv_cols)]
         dst = kvbuf.at[ds(u, seq_rows), ds(c, kv_cols)]
         return remote(src, dst, kv_send.at[c, k], kv_recv.at[c, u], {"uly": to})
 
@@ -202,23 +257,41 @@
     def out_own(c):
         return pltpu.make_async_copy(att.at[ds(u, seq_rows), ds(c, cols)], out_place(u, c), out_loc.at[c])
 
-    own_weights(0)
+    for c in range(min(AHEAD, chunks)):
+        own_weights(c)
     for k in range(2, n, 2):
         token_copy(k).start()
     token_mate().start()
+    raw_copy.wait()
+
+    heads = kv_in.shape[1]
+
+    def widen(t, carry):
+        part = kv_raw[ds(t, 16), :, :].astype(jnp.float32)
+        for half in range(2):
+            kv_wide[half, ds(t, 16 * heads), :] = part[
+                :, :, half * head_width:(half + 1) * head_width
+            ].reshape(16 * heads, head_width)
+        return carry
+
+    lax.fori_loop(0, seq_rows // 16, widen, 0)
+
+    def gather_head(h, carry):
+        for half in range(2):
+            rows = kv_wide[half, pl.ds(h, seq_rows, stride=heads), :]
+            kv_flat[:, ds(2 * h + half, head_width)] = rows.astype(jnp.bfloat16)
+        return carry
+
+    lax.fori_loop(0, heads, gather_head, 0)
     for k in range(1, n):
         kv_copy(0, k).start()
-    locals_ = (
-        pltpu.make_async_copy(w_in, wbuf.at[ds(b, shard), :], loc_sem.at[0]),
-        pltpu.make_async_copy(tok_in, token_rows(u), loc_sem.at[1]),
-        pltpu.make_async_copy(
-            kv_in.at[:, ds(u, kv_width)], kvbuf.at[ds(u, seq_rows), :], loc_sem.at[2]
-        ),
+    own_kv = pltpu.make_async_copy(
+        kv_flat.at[:, ds(u, kv_width)], kvbuf.at[ds(u, seq_rows), :], loc_sem.at[2]
     )
-    for copy in locals_:
-        copy.start()
-    for copy in locals_:
+    own_kv.start()
+    for copy in own_copies:
         copy.wait()
+    own_kv.wait()
 
     scale = head_width ** (-0.5)
     block = min(QUERY_ROWS, total_rows)
@@ -249,9 +322,9 @@
         lax.fori_loop(0, total_rows // block, rows_step, 0)
 
     def chunk_step(i, carry):
-        @pl.when(i + 1 < chunks)
-        def _():
-            own_weights(i + 1)
+        @pl.when(i + AHEAD < chunks)
+        def _():
+            own_weights(i + AHEAD)
 
         @pl.when(i < chunks)
         def _():
@@ -323,11 +396,16 @@
             pltpu.VMEM((total_rows, 2 * width), jnp.bfloat16),
             pltpu.VMEM((total_rows, width), jnp.bfloat16),
             pltpu.VMEM((total_rows, cols), jnp.bfloat16),
-            dma((3,)),
+            pltpu.VMEM((seq_rows, all_heads, 2 * head_width), jnp.bfloat16),
+            pltpu.VMEM((2, seq_rows * all_heads, head_width), jnp.float32),
+            pltpu.VMEM((seq_rows, all_heads * 2 * head_width), jnp.bfloat16),
+            dma((4,)),
             dma((n,)),
             dma((n,)),
             dma((n,)),
             dma((3, chunks, blocks)),
+            dma((chunks, blocks)),
+            dma((2, chunks, blocks)),
             dma((chunks, blocks)),
             dma((chunks, n)),
             dma((chunks, n)),
@@ -346,7 +424,7 @@
     )(
         tokens[0],
         query_weight.reshape(shard, width),
-        key_values[0].reshape(seq_rows, all_heads * 2 * head_width),
+        key_values[0],
     )
     return out.reshape(1, seq_rows, all_heads, head_width)
 

time: 92.8 us -> 121 us (1.30)
  Pallas kernels: 86.7 us -> 115 us
    pallas_call x1, Pallas kernels: 86.7 us -> 115 us  [body(): pl.pallas_call(functools.partial(kernel, n, blocks, head_width, chunks),...]
    unnamed x5 -> x6, local copies, waits for them, and re-layouts: 5.59 us -> 5.22 us
where the time goes in v2:
time: 121 us; the launch traced here: 120 us
  Pallas kernels  115 us (95%)
  local copies, waits for them, and re-layouts  5.22 us (4%)
    pallas_call x1, Pallas kernels, body(): pl.pallas_call(functools.partial(kernel, n, blocks, head_width, chunks),...  115 us
    unnamed x6, local copies, waits for them, and re-layouts  5.22 us

profile of v2, /device:TPU:0, one launch (start us, length us, event | category | flops | bytes accessed | tf_op | source)
XLA Modules:
  0.0 120.4 jit_solution(8111949113037546121)
XLA Ops:
  0.0 1.3 %copy.7 = bf16[48,8,8,128]{3,1,2,0:T(8,128)(2,1)S(1)} copy(bf16[48,8,8,128]{3,2,1,0:T(8,128)(2,1)} %bitcast.13) | data formatting | bytes 1572864
  1.3 0.0 copy-start
  1.3 1.6 %copy-done = bf16[1,128,32,256]{3,2,1,0:T(8,128)(2,1)S(1)} copy-done((bf16[1,128,32,256]{3,2,1,0:T(8,128)(2,1)S(1)}, bf16[1,128,32,256]{3,2,1,0:T(8,128)(2,1)}, u32[]{:S(2)}) %copy-start) | copy-done | bytes 2097176
  2.9 0.0 copy-start.1
  2.9 1.1 copy-done.1
  4.0 115.1 %shard_map.37 = bf16[128,4096]{1,0:T(8,128)(2,1)S(1)} custom-call(bf16[128,3072]{1,0:T(8,128)(2,1)S(1)} %bitcast.12, bf16[384,1024]{1,0:T(8,128)(2,1)S(1)} %bitcast.10, bf16[128,32,256]{2,1,0:T(8,128)(2,1)S(1)} %bitcast.11), custom_call_target="tpu_custom_call" | custom-call | flops 4294967296 | bytes 3670016 | tf_op jit(solution)/shard_map/pallas_call | solution.py:388
  119.2 1.2 copy.5
Async XLA Ops:
  1.3 1.6 %copy-start = (bf16[1,128,32,256]{3,2,1,0:T(8,128)(2,1)S(1)}, bf16[1,128,32,256]{3,2,1,0:T(8,128)(2,1)}, u32[]{:S(2)}) copy-start(bf16[1,128,32,256]{3,2,1,0:T(8,128)(2,1)} %param.5) | copy-start | bytes 6291460
  2.9 1.1 copy-start.1

commit v3 on v2

--- a/solution.py
+++ b/solution.py
@@ -8,8 +8,8 @@
 from jax.sharding import PartitionSpec as P
 
 MESH = pl.DeviceIdType.MESH
-CHUNK_HEADS = 1
-AHEAD = 2
+CHUNK_HEADS = 2
+AHEAD = 1
 QUERY_ROWS = 256
 
 
@@ -27,9 +27,6 @@
     kvbuf,
     att,
     qbuf,
-    kv_raw,
-    kv_wide,
-    kv_flat,
     loc_sem,
     tok_send,
     tok_fwd,
@@ -52,12 +49,10 @@
     mate = z * 2 + (1 - y)
     core_mate = u + 1 - 2 * (u % 2)
     seq_rows = tok_in.shape[0]
-    shard = w_in.shape[0]
-    width = w_in.shape[1]
-    cols = width // chunks
+    shard = w_in.shape[1]
+    heads = w_in.shape[0]
+    chunk_heads = heads // chunks
     side = max(16, shard // 6 // 16 * 16)
-    kv_width = 2 * width
-    kv_cols = 2 * cols
     total_rows = n * seq_rows
 
     def ds(start, size):
@@ -72,11 +67,12 @@
     has_up = z < line - 1
     has_down = z > 0
 
-    raw_copy = pltpu.make_async_copy(kv_in, kv_raw, loc_sem.at[3])
-    raw_copy.start()
     own_copies = (
-        pltpu.make_async_copy(w_in, wbuf.at[ds(b, shard), :], loc_sem.at[0]),
+        pltpu.make_async_copy(w_in, wbuf.at[:, ds(b, shard), :], loc_sem.at[0]),
         pltpu.make_async_copy(tok_in, tok.at[ds(u, seq_rows), :], loc_sem.at[1]),
+        pltpu.make_async_copy(
+            kv_in.at[ds(u, heads)], kvbuf.at[:, ds(u, seq_rows), :], loc_sem.at[2]
+        ),
     )
     for copy in own_copies:
         copy.start()
@@ -113,23 +109,25 @@
         pl.semaphore_wait(barrier, n)
 
     def piece(c, s):
-        return wbuf.at[ds(s, shard), ds(c, cols)]
+        return wbuf.at[ds(c, chunk_heads), ds(s, shard), :]
 
     UP, DOWN, ACROSS = 0, 1, 2
 
     def w_copy(c, s, way, own=False):
         step = (2, -2, 0)[way]
         device = mate if way == ACROSS else b + step
-        src = w_in.at[:, ds(c, cols)] if own else piece(c, s)
+        src = w_in.at[ds(c, chunk_heads)] if own else piece(c, s)
         return remote(src, piece(c, s), w_send.at[way, c, s], w_recv.at[c, s], {"blk": device})
 
     def main_copy(c, s):
         rows = pl.ds(pl.multiple_of(s * shard + side, 16), shard - side)
-        part = wbuf.at[rows, ds(c, cols)]
+        part = wbuf.at[ds(c, chunk_heads), rows, :]
         return remote(part, part, w_send.at[ACROSS, c, s], w_recv.at[c, s], {"blk": mate})
 
     def side_copy(c, s, way):
-        part = wbuf.at[pl.ds(pl.multiple_of(s * shard, 16), side), ds(c, cols)]
+        part = wbuf.at[
+            ds(c, chunk_heads), pl.ds(pl.multiple_of(s * shard, 16), side), :
+        ]
         device = b + (2, -2)[way]
         return remote(part, part, side_send.at[way, c, s], side_recv.at[c, s], {"blk": device})
 
@@ -232,66 +230,40 @@
 
     def kv_copy(c, k):
         to = (u + k) % n
-        src = kv_flat.at[:, pl.ds(pl.multiple_of(to * kv_width + c * kv_cols, kv_cols), kv_cols)]
-        dst = kvbuf.at[ds(u, seq_rows), ds(c, kv_cols)]
+        src = kv_in.at[pl.ds(to * heads + c * chunk_heads, chunk_heads)]
+        dst = kvbuf.at[ds(c, chunk_heads), ds(u, seq_rows), :]
         return remote(src, dst, kv_send.at[c, k], kv_recv.at[c, u], {"uly": to})
 
     def kv_arrival(c, k):
         s = (u + n - k) % n
-        dst = kvbuf.at[ds(s, seq_rows), ds(c, kv_cols)]
+        dst = kvbuf.at[ds(c, chunk_heads), ds(s, seq_rows), :]
         return remote(dst, dst, kv_send.at[c, k], kv_recv.at[c, s], {"uly": s})
 
     def out_place(s, c):
-        return out_ref.at[:, pl.ds(pl.multiple_of(s * width + c * cols, cols), cols)]
+        return out_ref.at[pl.ds(s * heads + c * chunk_heads, chunk_heads)]
 
     def out_copy(c, k):
         to = (u + k) % n
-        src = att.at[ds(to, seq_rows), ds(c, cols)]
+        src = att.at[ds(c, chunk_heads), ds(to, seq_rows), :]
         return remote(src, out_place(u, c), out_send.at[c, k], out_recv.at[c, u], {"uly": to})
 
     def out_arrival(c, k):
         s = (u + n - k) % n
-        src = att.at[ds(s, seq_rows), ds(c, cols)]
+        src = att.at[ds(c, chunk_heads), ds(s, seq_rows), :]
         return remote(src, out_place(s, c), out_send.at[c, k], out_recv.at[c, s], {"uly": s})
 
     def out_own(c):
-        return pltpu.make_async_copy(att.at[ds(u, seq_rows), ds(c, cols)], out_place(u, c), out_loc.at[c])
+        return pltpu.make_async_copy(att.at[ds(c, chunk_heads), ds(u, seq_rows), :], out_place(u, c), out_loc.at[c])
 
     for c in range(min(AHEAD, chunks)):
         own_weights(c)
     for k in range(2, n, 2):
         token_copy(k).start()
     token_mate().start()
-    raw_copy.wait()
-
-    heads = kv_in.shape[1]
-
-    def widen(t, carry):
-        part = kv_raw[ds(t, 16), :, :].astype(jnp.float32)
-        for half in range(2):
-            kv_wide[half, ds(t, 16 * heads), :] = part[
-                :, :, half * head_width:(half + 1) * head_width
-            ].reshape(16 * heads, head_width)
-        return carry
-
-    lax.fori_loop(0, seq_rows // 16, widen, 0)
-
-    def gather_head(h, carry):
-        for half in range(2):
-            rows = kv_wide[half, pl.ds(h, seq_rows, stride=heads), :]
-            kv_flat[:, ds(2 * h + half, head_width)] = rows.astype(jnp.bfloat16)
-        return carry
-
-    lax.fori_loop(0, heads, gather_head, 0)
     for k in range(1, n):
         kv_copy(0, k).start()
-    own_kv = pltpu.make_async_copy(
-        kv_flat.at[:, ds(u, kv_width)], kvbuf.at[ds(u, seq_rows), :], loc_sem.at[2]
-    )
-    own_kv.start()
     for copy in own_copies:
         copy.wait()
-    own_kv.wait()
 
     scale = head_width ** (-0.5)
     block = min(QUERY_ROWS, total_rows)
@@ -299,14 +271,17 @@
     def attend(c):
         def rows_step(r, carry):
             rows = pl.ds(pl.multiple_of(r * block, block), block)
+            weight = jnp.concatenate(
+                [wbuf[c * chunk_heads + h, :, :] for h in range(chunk_heads)], axis=1
+            )
             qbuf[rows, :] = jnp.dot(
-                tok[rows, :], wbuf[:, ds(c, cols)], preferred_element_type=jnp.float32
+                tok[rows, :], weight, preferred_element_type=jnp.float32
             ).astype(jnp.bfloat16)
-            for h in range(cols // head_width):
+            for h in range(chunk_heads):
                 q = qbuf[rows, h * head_width:(h + 1) * head_width]
-                at = c * kv_cols + 2 * h * head_width
-                k = kvbuf[:, pl.ds(pl.multiple_of(at, head_width), head_width)]
-                v = kvbuf[:, pl.ds(pl.multiple_of(at + head_width, head_width), head_width)]
+                at = c * chunk_heads + h
+                k = kvbuf[at, :, :head_width]
+                v = kvbuf[at, :, head_width:]
                 scores = lax.dot_general(
                     q, k, (((1,), (1,)), ((), ())), preferred_element_type=jnp.float32
                 ) * scale
@@ -315,8 +290,7 @@
                 weighted = jnp.dot(
                     soft.astype(jnp.bfloat16), v, preferred_element_type=jnp.float32
                 )
-                place = pl.ds(pl.multiple_of(c * cols + h * head_width, head_width), head_width)
-                att[rows, place] = (weighted / row_sum).astype(jnp.bfloat16)
+                att[at, rows, :] = (weighted / row_sum).astype(jnp.bfloat16)
             return carry
 
         lax.fori_loop(0, total_rows // block, rows_step, 0)
@@ -387,19 +361,16 @@
     flops = 2 * total_rows * width * (depth + 2 * total_rows)
     out = pl.pallas_call(
         functools.partial(kernel, n, blocks, head_width, chunks),
-        out_shape=jax.ShapeDtypeStruct((seq_rows, all_heads * head_width), jnp.bfloat16),
+        out_shape=jax.ShapeDtypeStruct((all_heads, seq_rows, head_width), jnp.bfloat16),
         in_specs=[pl.BlockSpec(memory_space=pl.ANY)] * 3,
         out_specs=pl.BlockSpec(memory_space=pl.ANY),
         scratch_shapes=[
             pltpu.VMEM((total_rows, depth), jnp.bfloat16),
-            pltpu.VMEM((depth, width), jnp.bfloat16),
-            pltpu.VMEM((total_rows, 2 * width), jnp.bfloat16),
-            pltpu.VMEM((total_rows, width), jnp.bfloat16),
+            pltpu.VMEM((heads, depth, head_width), jnp.bfloat16),
+            pltpu.VMEM((heads, total_rows, 2 * head_width), jnp.bfloat16),
+            pltpu.VMEM((heads, total_rows, head_width), jnp.bfloat16),
             pltpu.VMEM((total_rows, cols), jnp.bfloat16),
-            pltpu.VMEM((seq_rows, all_heads, 2 * head_width), jnp.bfloat16),
-            pltpu.VMEM((2, seq_rows * all_heads, head_width), jnp.float32),
-            pltpu.VMEM((seq_rows, all_heads * 2 * head_width), jnp.bfloat16),
-            dma((4,)),
+            dma((3,)),
             dma((n,)),
             dma((n,)),
             dma((n,)),
@@ -423,10 +394,10 @@
         ),
     )(
         tokens[0],
-        query_weight.reshape(shard, width),
-        key_values[0],
+        jnp.transpose(query_weight, (1, 0, 2)),
+        jnp.transpose(key_values[0], (1, 0, 2)),
     )
-    return out.reshape(1, seq_rows, all_heads, head_width)
+    return jnp.transpose(out, (1, 0, 2))[None]
 
 
 def solution(mesh):

time: 121 us -> 91.5 us (0.76)
  Pallas kernels: 115 us -> 85.5 us
    pallas_call x1, Pallas kernels: 115 us -> 85.5 us  [body(): pl.pallas_call(functools.partial(kernel, n, blocks, head_width, chunks),...]
    broadcast_in_dim x0 -> x1, local copies, waits for them, and re-layouts: none -> 1.65 us  [body(): return jnp.transpose(out, (1, 0, 2))[None]]
    unnamed x6 -> x4, local copies, waits for them, and re-layouts: 5.22 us -> 4.08 us
where the time goes in v3:
time: 91.5 us; the launch traced here: 91.3 us
  Pallas kernels  85.5 us (93%)
  local copies, waits for them, and re-layouts  5.73 us (6%)
    pallas_call x1, Pallas kernels, body(): pl.pallas_call(functools.partial(kernel, n, blocks, head_width, chunks),...  85.5 us
    unnamed x4, local copies, waits for them, and re-layouts  4.08 us

profile of v3, /device:TPU:0, one launch (start us, length us, event | category | flops | bytes accessed | tf_op | source)
XLA Modules:
  0.0 91.3 jit_solution(8265164427465547845)
XLA Ops:
  0.0 1.2 %copy.10 = bf16[384,8,128]{2,0,1:T(8,128)(2,1)S(1)} copy(bf16[384,8,128]{2,1,0:T(8,128)(2,1)} %param.4) | data formatting | bytes 1572864 | tf_op args[1]
  1.2 0.0 copy-start
  1.3 2.8 %copy.9 = bf16[1,128,32,256]{3,1,2,0:T(8,128)(2,1)S(1)} copy(bf16[1,128,32,256]{3,2,1,0:T(8,128)(2,1)} %param.5) | data formatting | bytes 4194304 | tf_op args[2]
  4.1 0.0 copy-done
  4.1 85.5 %shard_map.37 = bf16[32,128,128]{2,1,0:T(8,128)(2,1)S(1)} custom-call(bf16[128,3072]{1,0:T(8,128)(2,1)S(1)} %bitcast.15, bf16[8,384,128]{2,1,0:T(8,128)(2,1)S(1)} %bitcast.14, bf16[32,128,256]{2,1,0:T(8,128)(2,1)S(1)} %bitcast.12), custom_call_target="tpu_custom_call" | custom-call | flops 4294967296 | bytes 3670016 | tf_op jit(solution)/shard_map/pallas_call | solution.py:362
  89.6 1.6 %copy.6 = bf16[1,128,32,128]{3,2,1,0:T(8,128)(2,1)} copy(bf16[1,128,32,128]{3,1,2,0:T(8,128)(2,1)S(1)} %bitcast.13) | data formatting | bytes 2097152 | tf_op jit(solution)/shard_map/broadcast_in_dim | solution.py:400
Async XLA Ops:
  1.2 2.9 %copy-start = (bf16[1,128,3072]{2,1,0:T(8,128)(2,1)S(1)}, bf16[1,128,3072]{2,1,0:T(8,128)(2,1)}, u32[]{:S(2)}) copy-start(bf16[1,128,3072]{2,1,0:T(8,128)(2,1)} %param.3) | copy-start | bytes 2359300

commit v4 on v3

--- a/solution.py
+++ b/solution.py
@@ -9,7 +9,8 @@
 
 MESH = pl.DeviceIdType.MESH
 CHUNK_HEADS = 2
-AHEAD = 1
+AHEAD = 2
+LAG = 2
 QUERY_ROWS = 256
 
 
@@ -142,7 +143,7 @@
         def _():
             w_copy(c, b, DOWN, True).start()
 
-    def pass_on(c):
+    def pass_on(c, between):
         ways = lambda d: (
             (UP, -2 * d, z - d >= 0, has_up),
             (DOWN, 2 * d, z + d < line, has_down),
@@ -170,21 +171,33 @@
                     def _():
                         side_copy(c, mate + step, way).start()
 
-        main(1)
-        w_copy(c, mate, ACROSS).wait_recv()
-
-        @pl.when(has_up)
-        def _():
-            side_copy(c, mate, UP).start()
-
-        @pl.when(has_down)
-        def _():
-            side_copy(c, mate, DOWN).start()
-
+        def forward(*steps):
+            @pl.when(c < chunks)
+            def _():
+                for step in steps:
+                    step()
+
+        def first():
+            w_copy(c, mate, ACROSS).wait_recv()
+
+            @pl.when(has_up)
+            def _():
+                side_copy(c, mate, UP).start()
+
+            @pl.when(has_down)
+            def _():
+                side_copy(c, mate, DOWN).start()
+
+        forward(functools.partial(main, 1), first)
         for d in range(2, line):
-            main(d)
-            sides(d - 1)
-        sides(line - 1)
+            if between:
+                between.pop(0)()
+            forward(functools.partial(main, d), functools.partial(sides, d - 1))
+        if between:
+            between.pop(0)()
+        forward(lambda: sides(line - 1))
+        for unit in between:
+            unit()
 
     def across_arrived(c):
         for j in range(line):
@@ -268,43 +281,77 @@
     scale = head_width ** (-0.5)
     block = min(QUERY_ROWS, total_rows)
 
-    def attend(c):
+    def project(c):
+        weight = jnp.concatenate(
+            [wbuf[c * chunk_heads + h, :, :] for h in range(chunk_heads)], axis=1
+        )
+        if total_rows <= 512:
+            qbuf[...] = jnp.dot(
+                tok[...], weight, preferred_element_type=jnp.float32
+            ).astype(jnp.bfloat16)
+        else:
+            def rows_step(r, carry):
+                rows = ds(r, block)
+                qbuf[rows, :] = jnp.dot(
+                    tok[rows, :], weight, preferred_element_type=jnp.float32
+                ).astype(jnp.bfloat16)
+                return carry
+
+            lax.fori_loop(0, total_rows // block, rows_step, 0)
+
+    def attend(c, h):
+        at = c * chunk_heads + h
+
         def rows_step(r, carry):
-            rows = pl.ds(pl.multiple_of(r * block, block), block)
-            weight = jnp.concatenate(
-                [wbuf[c * chunk_heads + h, :, :] for h in range(chunk_heads)], axis=1
-            )
-            qbuf[rows, :] = jnp.dot(
-                tok[rows, :], weight, preferred_element_type=jnp.float32
-            ).astype(jnp.bfloat16)
-            for h in range(chunk_heads):
-                q = qbuf[rows, h * head_width:(h + 1) * head_width]
-                at = c * chunk_heads + h
-                k = kvbuf[at, :, :head_width]
-                v = kvbuf[at, :, head_width:]
-                scores = lax.dot_general(
-                    q, k, (((1,), (1,)), ((), ())), preferred_element_type=jnp.float32
-                ) * scale
-                soft = jnp.exp(scores - jnp.max(scores, axis=1, keepdims=True))
-                row_sum = jnp.sum(soft, axis=1, keepdims=True)
-                weighted = jnp.dot(
-                    soft.astype(jnp.bfloat16), v, preferred_element_type=jnp.float32
-                )
-                att[at, rows, :] = (weighted / row_sum).astype(jnp.bfloat16)
+            rows = ds(r, block)
+            q = qbuf[rows, h * head_width:(h + 1) * head_width]
+            k = kvbuf[at, :, :head_width]
+            v = kvbuf[at, :, head_width:]
+            scores = lax.dot_general(
+                q, k, (((1,), (1,)), ((), ())), preferred_element_type=jnp.float32
+            ) * scale
+            soft = jnp.exp(scores - jnp.max(scores, axis=1, keepdims=True))
+            row_sum = jnp.sum(soft, axis=1, keepdims=True)
+            weighted = jnp.dot(soft.astype(jnp.bfloat16), v, preferred_element_type=jnp.float32)
+            att[at, rows, :] = (weighted / row_sum).astype(jnp.bfloat16)
             return carry
 
         lax.fori_loop(0, total_rows // block, rows_step, 0)
 
     def chunk_step(i, carry):
+        c = i - LAG
+
+        def unit(*steps):
+            def run():
+                @pl.when(c >= 0)
+                def _():
+                    for step in steps:
+                        step()
+
+            return run
+
+        def ready():
+            across_arrived(c)
+            for k in range(1, n):
+                kv_arrival(c, k).wait_recv()
+
+        def give_back():
+            for k in range(1, n):
+                out_copy(c, k).start()
+            out_own(c).start()
+
+        units = [unit(ready, lambda: project(c))]
+        for h in range(chunk_heads):
+            units.append(unit(functools.partial(attend, c, h)))
+
         @pl.when(i + AHEAD < chunks)
         def _():
             own_weights(i + AHEAD)
 
-        @pl.when(i < chunks)
-        def _():
-            pass_on(i)
-
-        @pl.when(i == 0)
+        pass_on(i, units)
+        unit(give_back)()
+
+        @pl.when(i == 1)
         def _():
             for k in range(2, n, 2):
                 token_arrival((u + n - k) % n).wait_recv()
@@ -317,20 +364,9 @@
             for k in range(1, n):
                 kv_copy(i + 1, k).start()
 
-        @pl.when(i > 0)
-        def _():
-            c = i - 1
-            across_arrived(c)
-            for k in range(1, n):
-                kv_arrival(c, k).wait_recv()
-            attend(c)
-            for k in range(1, n):
-                out_copy(c, k).start()
-            out_own(c).start()
-
         return carry
 
-    lax.fori_loop(0, chunks + 1, chunk_step, 0)
+    lax.fori_loop(0, chunks + LAG, chunk_step, 0)
 
     def drain(c, carry):
         weights_sent(c)

time: 91.5 us -> 87.1 us (0.952)
  Pallas kernels: 85.5 us -> 81.1 us
    pallas_call x1, Pallas kernels: 85.5 us -> 81.1 us  [body(): pl.pallas_call(functools.partial(kernel, n, blocks, head_width, chunks),...]
where the time goes in v4:
time: 87.1 us; the launch traced here: 86.9 us
  Pallas kernels  81.1 us (93%)
  local copies, waits for them, and re-layouts  5.73 us (7%)
    pallas_call x1, Pallas kernels, body(): pl.pallas_call(functools.partial(kernel, n, blocks, head_width, chunks),...  81.1 us
    unnamed x4, local copies, waits for them, and re-layouts  4.08 us

profile of v4, /device:TPU:0, one launch (start us, length us, event | category | flops | bytes accessed | tf_op | source)
XLA Modules:
  0.0 86.9 jit_solution(5701691174666421886)
XLA Ops:
  0.0 1.2 %copy.10 = bf16[384,8,128]{2,0,1:T(8,128)(2,1)S(1)} copy(bf16[384,8,128]{2,1,0:T(8,128)(2,1)} %param.4) | data formatting | bytes 1572864 | tf_op args[1]
  1.2 0.0 copy-start
  1.3 2.8 %copy.9 = bf16[1,128,32,256]{3,1,2,0:T(8,128)(2,1)S(1)} copy(bf16[1,128,32,256]{3,2,1,0:T(8,128)(2,1)} %param.5) | data formatting | bytes 4194304 | tf_op args[2]
  4.1 0.0 copy-done
  4.1 81.1 %shard_map.37 = bf16[32,128,128]{2,1,0:T(8,128)(2,1)S(1)} custom-call(bf16[128,3072]{1,0:T(8,128)(2,1)S(1)} %bitcast.15, bf16[8,384,128]{2,1,0:T(8,128)(2,1)S(1)} %bitcast.14, bf16[32,128,256]{2,1,0:T(8,128)(2,1)S(1)} %bitcast.12), custom_call_target="tpu_custom_call" | custom-call | flops 4294967296 | bytes 3670016 | tf_op jit(solution)/shard_map/pallas_call | solution.py:398
  85.2 1.6 %copy.6 = bf16[1,128,32,128]{3,2,1,0:T(8,128)(2,1)} copy(bf16[1,128,32,128]{3,1,2,0:T(8,128)(2,1)S(1)} %bitcast.13) | data formatting | bytes 2097152 | tf_op jit(solution)/shard_map/broadcast_in_dim | solution.py:436
Async XLA Ops:
  1.2 2.9 %copy-start = (bf16[1,128,3072]{2,1,0:T(8,128)(2,1)S(1)}, bf16[1,128,3072]{2,1,0:T(8,128)(2,1)}, u32[]{:S(2)}) copy-start(bf16[1,128,3072]{2,1,0:T(8,128)(2,1)} %param.3) | copy-start | bytes 2359300

commit v5 on v4

--- a/solution.py
+++ b/solution.py
@@ -10,7 +10,7 @@
 MESH = pl.DeviceIdType.MESH
 CHUNK_HEADS = 2
 AHEAD = 2
-LAG = 2
+LAG = 1
 QUERY_ROWS = 256
 
 
@@ -252,21 +252,21 @@
         dst = kvbuf.at[ds(c, chunk_heads), ds(s, seq_rows), :]
         return remote(dst, dst, kv_send.at[c, k], kv_recv.at[c, s], {"uly": s})
 
-    def out_place(s, c):
-        return out_ref.at[pl.ds(s * heads + c * chunk_heads, chunk_heads)]
-
-    def out_copy(c, k):
+    def out_copy(at, k):
         to = (u + k) % n
-        src = att.at[ds(c, chunk_heads), ds(to, seq_rows), :]
-        return remote(src, out_place(u, c), out_send.at[c, k], out_recv.at[c, u], {"uly": to})
-
-    def out_arrival(c, k):
+        src = att.at[at, ds(to, seq_rows), :]
+        dst = out_ref.at[u * heads + at]
+        return remote(src, dst, out_send.at[at, k], out_recv.at[at, u], {"uly": to})
+
+    def out_arrival(at, k):
         s = (u + n - k) % n
-        src = att.at[ds(c, chunk_heads), ds(s, seq_rows), :]
-        return remote(src, out_place(s, c), out_send.at[c, k], out_recv.at[c, s], {"uly": s})
-
-    def out_own(c):
-        return pltpu.make_async_copy(att.at[ds(c, chunk_heads), ds(u, seq_rows), :], out_place(u, c), out_loc.at[c])
+        src = att.at[at, ds(s, seq_rows), :]
+        dst = out_ref.at[s * heads + at]
+        return remote(src, dst, out_send.at[at, k], out_recv.at[at, s], {"uly": s})
+
+    def out_own(at):
+        src = att.at[at, ds(u, seq_rows), :]
+        return pltpu.make_async_copy(src, out_ref.at[u * heads + at], out_loc.at[at])
 
     for c in range(min(AHEAD, chunks)):
         own_weights(c)
@@ -317,6 +317,9 @@
             return carry
 
         lax.fori_loop(0, total_rows // block, rows_step, 0)
+        for k in range(1, n):
+            out_copy(at, k).start()
+        out_own(at).start()
 
     def chunk_step(i, carry):
         c = i - LAG
@@ -330,17 +333,24 @@
 
             return run
 
+        def token_pass():
+            @pl.when(c == 0)
+            def _():
+                for k in range(2, n, 2):
+                    token_arrival((u + n - k) % n).wait_recv()
+                    token_forward(k).start()
+
         def ready():
+            @pl.when(c == 0)
+            def _():
+                for k in range(1, n, 2):
+                    token_arrival((u + n - k) % n).wait_recv()
+
             across_arrived(c)
             for k in range(1, n):
                 kv_arrival(c, k).wait_recv()
 
-        def give_back():
-            for k in range(1, n):
-                out_copy(c, k).start()
-            out_own(c).start()
-
-        units = [unit(ready, lambda: project(c))]
+        units = [unit(token_pass), unit(ready, lambda: project(c))]
         for h in range(chunk_heads):
             units.append(unit(functools.partial(attend, c, h)))
 
@@ -349,16 +359,6 @@
             own_weights(i + AHEAD)
 
         pass_on(i, units)
-        unit(give_back)()
-
-        @pl.when(i == 1)
-        def _():
-            for k in range(2, n, 2):
-                token_arrival((u + n - k) % n).wait_recv()
-                token_forward(k).start()
-            for k in range(1, n, 2):
-                token_arrival((u + n - k) % n).wait_recv()
-
         @pl.when(i + 1 < chunks)
         def _():
             for k in range(1, n):
@@ -372,9 +372,12 @@
         weights_sent(c)
         for k in range(1, n):
             kv_copy(c, k).wait_send()
-            out_copy(c, k).wait_send()
-            out_arrival(c, k).wait_recv()
-        out_own(c).wait()
+        for h in range(chunk_heads):
+            at = c * chunk_heads + h
+            for k in range(1, n):
+                out_copy(at, k).wait_send()
+                out_arrival(at, k).wait_recv()
+            out_own(at).wait()
         return carry
 
     lax.fori_loop(0, chunks, drain, 0)
@@ -416,9 +419,9 @@
             dma((chunks, blocks)),
             dma((chunks, n)),
             dma((chunks, n)),
-            dma((chunks, n)),
-            dma((chunks, n)),
-            dma((chunks,)),
+            dma((heads, n)),
+            dma((heads, n)),
+            dma((heads,)),
         ],
         compiler_params=pltpu.CompilerParams(
             collective_id=0, has_side_effects=True, vmem_limit_bytes=48 * 1024 * 1024

time: 87.1 us -> 85.3 us (0.979)
  Pallas kernels: 81.1 us -> 79.4 us
    pallas_call x1, Pallas kernels: 81.1 us -> 79.4 us  [body(): pl.pallas_call(functools.partial(kernel, n, blocks, head_width, chunks),...]
where the time goes in v5:
time: 85.3 us; the launch traced here: 85.2 us
  Pallas kernels  79.4 us (93%)
  local copies, waits for them, and re-layouts  5.73 us (7%)
    pallas_call x1, Pallas kernels, body(): pl.pallas_call(functools.partial(kernel, n, blocks, head_width, chunks),...  79.4 us
    unnamed x4, local copies, waits for them, and re-layouts  4.08 us

profile of v5, /device:TPU:0, one launch (start us, length us, event | category | flops | bytes accessed | tf_op | source)
XLA Modules:
  0.0 85.2 jit_solution(1651159692863879207)
XLA Ops:
  0.0 1.2 %copy.10 = bf16[384,8,128]{2,0,1:T(8,128)(2,1)S(1)} copy(bf16[384,8,128]{2,1,0:T(8,128)(2,1)} %param.4) | data formatting | bytes 1572864 | tf_op args[1]
  1.2 0.0 copy-start
  1.3 2.8 %copy.9 = bf16[1,128,32,256]{3,1,2,0:T(8,128)(2,1)S(1)} copy(bf16[1,128,32,256]{3,2,1,0:T(8,128)(2,1)} %param.5) | data formatting | bytes 4194304 | tf_op args[2]
  4.1 0.0 copy-done
  4.1 79.4 %shard_map.37 = bf16[32,128,128]{2,1,0:T(8,128)(2,1)S(1)} custom-call(bf16[128,3072]{1,0:T(8,128)(2,1)S(1)} %bitcast.15, bf16[8,384,128]{2,1,0:T(8,128)(2,1)S(1)} %bitcast.14, bf16[32,128,256]{2,1,0:T(8,128)(2,1)S(1)} %bitcast.12), custom_call_target="tpu_custom_call" | custom-call | flops 4294967296 | bytes 3670016 | tf_op jit(solution)/shard_map/pallas_call | solution.py:401
  83.5 1.6 %copy.6 = bf16[1,128,32,128]{3,2,1,0:T(8,128)(2,1)} copy(bf16[1,128,32,128]{3,1,2,0:T(8,128)(2,1)S(1)} %bitcast.13) | data formatting | bytes 2097152 | tf_op jit(solution)/shard_map/broadcast_in_dim | solution.py:439
Async XLA Ops:
  1.2 2.9 %copy-start = (bf16[1,128,3072]{2,1,0:T(8,128)(2,1)S(1)}, bf16[1,128,3072]{2,1,0:T(8,128)(2,1)}, u32[]{:S(2)}) copy-start(bf16[1,128,3072]{2,1,0:T(8,128)(2,1)} %param.3) | copy-start | bytes 2359300

commit v6 on v5

--- a/solution.py
+++ b/solution.py
@@ -28,6 +28,9 @@
     kvbuf,
     att,
     qbuf,
+    kv_raw,
+    kv_wide,
+    kv_flat,
     loc_sem,
     tok_send,
     tok_fwd,
@@ -71,9 +74,7 @@
     own_copies = (
         pltpu.make_async_copy(w_in, wbuf.at[:, ds(b, shard), :], loc_sem.at[0]),
         pltpu.make_async_copy(tok_in, tok.at[ds(u, seq_rows), :], loc_sem.at[1]),
-        pltpu.make_async_copy(
-            kv_in.at[ds(u, heads)], kvbuf.at[:, ds(u, seq_rows), :], loc_sem.at[2]
-        ),
+        pltpu.make_async_copy(kv_in, kv_raw, loc_sem.at[2]),
     )
     for copy in own_copies:
         copy.start()
@@ -243,7 +244,7 @@
 
     def kv_copy(c, k):
         to = (u + k) % n
-        src = kv_in.at[pl.ds(to * heads + c * chunk_heads, chunk_heads)]
+        src = kv_flat.at[pl.ds(to * heads + c * chunk_heads, chunk_heads)]
         dst = kvbuf.at[ds(c, chunk_heads), ds(u, seq_rows), :]
         return remote(src, dst, kv_send.at[c, k], kv_recv.at[c, u], {"uly": to})
 
@@ -273,10 +274,38 @@
     for k in range(2, n, 2):
         token_copy(k).start()
     token_mate().start()
-    for k in range(1, n):
-        kv_copy(0, k).start()
     for copy in own_copies:
         copy.wait()
+
+    all_heads = kv_in.shape[1]
+    own_kv = pltpu.make_async_copy(
+        kv_flat.at[ds(u, heads)], kvbuf.at[:, ds(u, seq_rows), :], loc_sem.at[3]
+    )
+
+    def widen():
+        def rows_step(t, carry):
+            part = kv_raw[ds(t, 16), :, :].astype(jnp.float32)
+            for half in range(2):
+                kv_wide[half, ds(t, 16 * all_heads), :] = part[
+                    :, :, half * head_width:(half + 1) * head_width
+                ].reshape(16 * all_heads, head_width)
+            return carry
+
+        lax.fori_loop(0, seq_rows // 16, rows_step, 0)
+
+    def gather(start, stop):
+        def head_step(h, carry):
+            for half in range(2):
+                rows = kv_wide[half, pl.ds(h, seq_rows, stride=all_heads), :]
+                kv_flat[h, :, half * head_width:(half + 1) * head_width] = rows.astype(jnp.bfloat16)
+            return carry
+
+        lax.fori_loop(start, stop, head_step, 0)
+
+    def send_first():
+        own_kv.start()
+        for k in range(1, n):
+            kv_copy(0, k).start()
 
     scale = head_width ** (-0.5)
     block = min(QUERY_ROWS, total_rows)
@@ -324,8 +353,14 @@
     def chunk_step(i, carry):
         c = i - LAG
 
-        def unit(*steps):
+        def unit(*steps, opening=()):
             def run():
+                if opening:
+                    @pl.when(i == 0)
+                    def _():
+                        for step in opening:
+                            step()
+
                 @pl.when(c >= 0)
                 def _():
                     for step in steps:
@@ -345,13 +380,22 @@
             def _():
                 for k in range(1, n, 2):
                     token_arrival((u + n - k) % n).wait_recv()
+                own_kv.wait()
 
             across_arrived(c)
             for k in range(1, n):
                 kv_arrival(c, k).wait_recv()
 
-        units = [unit(token_pass), unit(ready, lambda: project(c))]
-        for h in range(chunk_heads):
+        middle = all_heads // 2
+        units = [
+            unit(token_pass, opening=(widen,)),
+            unit(ready, lambda: project(c), opening=(lambda: gather(0, middle),)),
+            unit(
+                functools.partial(attend, c, 0),
+                opening=(lambda: gather(middle, all_heads), send_first),
+            ),
+        ]
+        for h in range(1, chunk_heads):
             units.append(unit(functools.partial(attend, c, h)))
 
         @pl.when(i + AHEAD < chunks)
@@ -409,7 +453,10 @@
             pltpu.VMEM((heads, total_rows, 2 * head_width), jnp.bfloat16),
             pltpu.VMEM((heads, total_rows, head_width), jnp.bfloat16),
             pltpu.VMEM((total_rows, cols), jnp.bfloat16),
-            dma((3,)),
+            pltpu.VMEM((seq_rows, all_heads, 2 * head_width), jnp.bfloat16),
+            pltpu.VMEM((2, seq_rows * all_heads, head_width), jnp.float32),
+            pltpu.VMEM((all_heads, seq_rows, 2 * head_width), jnp.bfloat16),
+            dma((4,)),
             dma((n,)),
             dma((n,)),
             dma((n,)),
@@ -424,7 +471,7 @@
             dma((heads,)),
         ],
         compiler_params=pltpu.CompilerParams(
-            collective_id=0, has_side_effects=True, vmem_limit_bytes=48 * 1024 * 1024
+            collective_id=0, has_side_effects=True, vmem_limit_bytes=60 * 1024 * 1024
         ),
         cost_estimate=pl.CostEstimate(
             flops=flops,
@@ -434,7 +481,7 @@
     )(
         tokens[0],
         jnp.transpose(query_weight, (1, 0, 2)),
-        jnp.transpose(key_values[0], (1, 0, 2)),
+        key_values[0],
     )
     return jnp.transpose(out, (1, 0, 2))[None]
 

time: 85.3 us -> 83.9 us (0.984)
    unnamed x4 -> x1, local copies, waits for them, and re-layouts: 4.08 us -> 2.11 us
    broadcast_in_dim x1, local copies, waits for them, and re-layouts: 1.65 us -> 2.87 us  [body(): return jnp.transpose(out, (1, 0, 2))[None]]
where the time goes in v6:
time: 83.9 us; the launch traced here: 83.8 us
  Pallas kernels  78.8 us (94%)
  local copies, waits for them, and re-layouts  4.99 us (6%)
    pallas_call x1, Pallas kernels, body(): pl.pallas_call(functools.partial(kernel, n, blocks, head_width, chunks),...  78.8 us
    broadcast_in_dim x1, local copies, waits for them, and re-layouts, body(): return jnp.transpose(out, (1, 0, 2))[None]  2.87 us
    unnamed x1, local copies, waits for them, and re-layouts  2.11 us

profile of v6, /device:TPU:0, one launch (start us, length us, event | category | flops | bytes accessed | tf_op | source)
XLA Modules:
  0.0 83.8 jit_solution(12968598289680000054)
XLA Ops:
  0.0 2.1 %copy.7 = bf16[384,8,128]{2,0,1:T(8,128)(2,1)} copy(bf16[384,8,128]{2,1,0:T(8,128)(2,1)} %param.4) | data formatting | bytes 1572864 | tf_op args[1]
  2.1 78.8 %shard_map.37 = bf16[32,128,128]{2,1,0:T(8,128)(2,1)} custom-call(bf16[128,3072]{1,0:T(8,128)(2,1)} %bitcast.11, bf16[8,384,128]{2,1,0:T(8,128)(2,1)} %bitcast.9, bf16[128,32,256]{2,1,0:T(8,128)(2,1)} %bitcast.10), custom_call_target="tpu_custom_call" | custom-call | flops 4294967296 | bytes 3670016 | tf_op jit(solution)/shard_map/pallas_call | solution.py:445
  80.9 2.9 %copy.5 = bf16[1,128,32,128]{3,2,1,0:T(8,128)(2,1)} copy(bf16[1,128,32,128]{3,1,2,0:T(8,128)(2,1)} %bitcast.8) | data formatting | bytes 2097152 | tf_op jit(solution)/shard_map/broadcast_in_dim | solution.py:486

commit v7 on v6

--- a/solution.py
+++ b/solution.py
@@ -471,7 +471,7 @@
             dma((heads,)),
         ],
         compiler_params=pltpu.CompilerParams(
-            collective_id=0, has_side_effects=True, vmem_limit_bytes=60 * 1024 * 1024
+            collective_id=0, has_side_effects=True, vmem_limit_bytes=51 * 1024 * 1024
         ),
         cost_estimate=pl.CostEstimate(
             flops=flops,

time: 83.9 us -> 83 us (0.989)
  local copies, waits for them, and re-layouts: 4.99 us -> 4.01 us
    broadcast_in_dim x1, local copies, waits for them, and re-layouts: 2.87 us -> 1.65 us  [body(): return jnp.transpose(out, (1, 0, 2))[None]]
    unnamed x1 -> x3, local copies, waits for them, and re-layouts: 2.11 us -> 2.36 us
where the time goes in v7:
time: 83 us; the launch traced here: 82.8 us
  Pallas kernels  78.8 us (95%)
  local copies, waits for them, and re-layouts  4.01 us (5%)
    pallas_call x1, Pallas kernels, body(): pl.pallas_call(functools.partial(kernel, n, blocks, head_width, chunks),...  78.8 us
    unnamed x3, local copies, waits for them, and re-layouts  2.36 us

profile of v7, /device:TPU:0, one launch (start us, length us, event | category | flops | bytes accessed | tf_op | source)
XLA Modules:
  0.0 82.8 jit_solution(2050828950049668676)
XLA Ops:
  0.0 1.2 %copy.7 = bf16[384,8,128]{2,0,1:T(8,128)(2,1)S(1)} copy(bf16[384,8,128]{2,1,0:T(8,128)(2,1)} %param.4) | data formatting | bytes 1572864 | tf_op args[1]
  1.2 0.0 copy-start
  1.3 1.1 %copy-done = bf16[1,128,3072]{2,1,0:T(8,128)(2,1)S(1)} copy-done((bf16[1,128,3072]{2,1,0:T(8,128)(2,1)S(1)}, bf16[1,128,3072]{2,1,0:T(8,128)(2,1)}, u32[]{:S(2)}) %copy-start) | copy-done | bytes 786456
  2.4 78.8 %shard_map.37 = bf16[32,128,128]{2,1,0:T(8,128)(2,1)S(1)} custom-call(bf16[128,3072]{1,0:T(8,128)(2,1)S(1)} %bitcast.10, bf16[8,384,128]{2,1,0:T(8,128)(2,1)S(1)} %bitcast.9, bf16[128,32,256]{2,1,0:T(8,128)(2,1)} %bitcast.11), custom_call_target="tpu_custom_call" | custom-call | flops 4294967296 | bytes 3670016 | tf_op jit(solution)/shard_map/pallas_call | solution.py:445
  81.2 1.6 %copy.5 = bf16[1,128,32,128]{3,2,1,0:T(8,128)(2,1)} copy(bf16[1,128,32,128]{3,1,2,0:T(8,128)(2,1)S(1)} %bitcast.8) | data formatting | bytes 2097152 | tf_op jit(solution)/shard_map/broadcast_in_dim | solution.py:486
Async XLA Ops:
  1.2 1.1 %copy-start = (bf16[1,128,3072]{2,1,0:T(8,128)(2,1)S(1)}, bf16[1,128,3072]{2,1,0:T(8,128)(2,1)}, u32[]{:S(2)}) copy-start(bf16[1,128,3072]{2,1,0:T(8,128)(2,1)} %param.3) | copy-start | bytes 2359300
